TPU v7x, 256 devices: a whole 4x4x8 slice. The times are simulated.
256 devices in a mesh: ta: 8 (over y, z_lo), sa: 32 (over z_hi, x, core).
Axes of the slice: x: 4, y: 4, z: 8 (z_hi: 4, z_lo: 2; z = z_hi * 2 + z_lo), core: 2. Of those that a mesh axis runs over, the one named last changes fastest.
Arguments:
- series: float32 [512, 65536], P('sa', 'ta'), may hold values from -6 to 6
- index_series: float32 [16, 65536], P(None, 'ta'), may hold values from -6 to 6
- assign: int32 [512], replicated, may hold values from 0 to 15
Outputs:
- autocorr: float32 [512, 4096], P('sa', 'ta')
- crosscorr: float32 [512, 4096], P('sa', 'ta')
Inputs may be any that keep to these rules, and one draw needn't show every extreme that they name: `assign`: each series names one index series.
All inputs are finite; a program needn't handle non-finite values.
Results may differ from a plain program's by a relative error of at most 0.000098.
Values sent between devices are 32-bit elements; how exact they have to be, the bound alone decides.
No kernel may reach another device: no remote copies, remote signals or barrier semaphores. Data moves between devices by JAX's collectives and lax.ppermute only.
A program may use at most 64 MiB of HBM per device.

v0:
```python
import functools
import math

import jax
import jax.numpy as jnp
import numpy as np
from jax import lax
from jax.experimental import pallas as pl
from jax.experimental.pallas import tpu as pltpu
from jax.sharding import PartitionSpec as P

LANES = 128
ROWS = 32
BLOCK = ROWS * LANES
FFT = 2 * BLOCK
BF16 = jnp.bfloat16
F32 = jnp.float32
W1 = 1024
W4 = W1 + 64
SPLITS = (0, 6, 12, 16)
TW = W4 + ROWS


def twiddle(wide, i):
    return sum(
        wide[TW + (p * 3 + i // 2) * ROWS : TW + (p * 3 + i // 2 + 1) * ROWS, i % 2 * LANES : (i % 2 + 1) * LANES].astype(F32)
        for p in (2, 1, 0)
    )


def split_np(table):
    hi = table.astype(np.float32).astype(BF16)
    lo = (table - hi.astype(np.float64)).astype(np.float32).astype(BF16)
    return hi, lo


def tables():
    k1 = np.arange(ROWS)[:, None] + 0.5
    t1 = np.arange(ROWS)[None, :]
    first = 2.0 * math.pi * k1 * t1 / (2 * ROWS)
    w1 = np.concatenate([np.cos(first), -np.sin(first)], axis=0)
    w1_hi, w1_lo = split_np(w1)
    w1 = np.concatenate([w1_hi, w1_lo, w1_hi], axis=1)
    t2 = np.arange(LANES)[None, :]
    turn = 2.0 * math.pi * k1 * t2 / FFT
    sign = np.where(np.arange(ROWS) % 2 == 0, 1.0, -1.0)[:, None] * np.ones((1, LANES))
    twiddles = np.stack([np.cos(turn), np.sin(turn), np.sin(turn) * sign, -np.cos(turn) * sign, sign])
    second = 2.0 * math.pi * np.arange(LANES)[:, None] * np.arange(LANES)[None, :] / LANES
    c, s = np.cos(second), np.sin(second)
    fwd = np.concatenate([np.concatenate([c, -s], 1), np.concatenate([s, c], 1)], 0)
    inv = np.concatenate([np.concatenate([c, s], 1), np.concatenate([-s, c], 1)], 0)
    n1 = np.arange(ROWS).reshape(8, 4).T.reshape(-1)[:, None]
    last = 2.0 * math.pi * (np.arange(ROWS)[None, :] + 0.5) * n1 / (2 * ROWS)
    w4 = np.concatenate([np.cos(last), -np.sin(last)], axis=1) * (2.0 / FFT / 256.0)
    w4_hi, w4_lo = split_np(w4)
    w4 = np.concatenate([w4_hi, w4_lo, w4_hi], axis=1)
    wide = np.zeros((TW + 9 * ROWS, 2 * LANES), BF16)
    wide[:512] = np.concatenate(split_np(fwd))
    wide[512:1024] = np.concatenate(split_np(inv))
    wide[W1 : W1 + 64, :96] = w1
    wide[W4 : W4 + ROWS, :192] = w4
    rest = twiddles.astype(np.float32)
    for piece in range(3):
        part = rest.astype(BF16)
        rest = rest - part.astype(np.float32)
        for i in range(5):
            at = TW + (piece * 3 + i // 2) * ROWS
            wide[at : at + ROWS, i % 2 * LANES : (i % 2 + 1) * LANES] = part[i]
    return wide


def split(value):
    hi = value.astype(BF16)
    return hi, (value - hi.astype(F32)).astype(BF16)


def dot(a, b):
    return jnp.dot(a, b, preferred_element_type=F32)


def first_stage(blocks, w1, tw_c, tw_s):
    hi, lo = split(jnp.concatenate(blocks, axis=1))
    both = dot(w1, jnp.concatenate([hi, hi, lo], axis=0))
    done = []
    for i in range(2):
        re = both[:ROWS, i * LANES : (i + 1) * LANES]
        im = both[ROWS:, i * LANES : (i + 1) * LANES]
        done.append(jnp.concatenate([re * tw_c + im * tw_s, im * tw_c - re * tw_s], axis=1))
    return done


def second_stage(value, f_hi, f_lo):
    hi, lo = split(value)
    return dot(jnp.concatenate([hi, lo, hi], axis=1), jnp.concatenate([f_hi, f_hi, f_lo], axis=0))


def parts(value):
    return value[:, :LANES], value[:, LANES:]


def mul_conj(a, b):
    (ar, ai), (br, bi) = a, b
    return ar * br + ai * bi, ai * br - ar * bi


def forward(ref, starts, w1, tw_c, tw_s, f_hi, f_lo):
    staged = []
    for i in range(0, len(starts), 2):
        blocks = [ref[pl.ds(start, ROWS, stride=8), :] for start in starts[i : i + 2]]
        staged += first_stage(blocks, w1, tw_c, tw_s)
    return second_stage(jnp.concatenate(staged, axis=0), f_hi, f_lo)


def tails(source, step, series, target):
    for i, s in enumerate(series):
        target[pl.ds(i * ROWS, ROWS), :] = source[pl.ds(step * (s // 8) + step - 256 + s % 8, ROWS, stride=8), :]


def tails_kernel(series, x_ref, *refs):
    tails(x_ref, 512, series, refs[-1])


def block_start(s, b):
    return (s // 8) * 512 + s % 8 + b * 256


def local_kernel(assign_ref, x_ref, y_ref, wide, pre_ref, x0_ref, y0_ref, ys_ref):
    base = lax.axis_index("sa") * 16
    w1 = wide[W1 : W1 + 64, :96]
    tw_c, tw_s, sign = (twiddle(wide, i) for i in (0, 1, 4))
    f_hi, f_lo = wide[:256], wide[256:512]
    group = 4

    def spectra(ref, g):
        starts = [block_start(s, b) for s in range(g, g + group) for b in range(2)]
        return forward(ref, starts, w1, tw_c, tw_s, f_hi, f_lo)

    for g in range(0, 16, group):
        ys_ref[pl.ds(g * 64, group * 64), :] = spectra(y_ref, g)
    for g in range(0, 16, group):
        spec = spectra(x_ref, g)
        for i in range(group):
            s = g + i
            x0 = spec[i * 64 : i * 64 + ROWS]
            x1 = parts(spec[i * 64 + ROWS : i * 64 + 64])
            x0_ref[s] = x0
            x0 = parts(x0)
            at = pl.multiple_of(assign_ref[base + s] * 64, 64)
            y0 = ys_ref[pl.ds(at, ROWS), :]
            y1 = parts(ys_ref[pl.ds(at + ROWS, ROWS), :])
            y0_ref[s] = y0
            y0 = parts(y0)
            window = (x1[0] - sign * x0[1], x1[1] + sign * x0[0])
            re, im = mul_conj(x1, window)
            pre_ref[s, 0] = jnp.concatenate([re + x0[0] * x0[0] + x0[1] * x0[1], im], axis=1)
            re, im = mul_conj(y1, window)
            re0, im0 = mul_conj(y0, x0)
            pre_ref[s, 1] = jnp.concatenate([re + re0, im + im0], axis=1)


def halo_kernel(series, h_ref, pre_ref, x0_ref, y0_ref, wide, *refs):
    out_ref = refs[-1]
    w1 = wide[W1 : W1 + 64, :96]
    w4 = wide[W4 : W4 + ROWS, :192]
    tw_c, tw_s, twh_c, twh_s = (twiddle(wide, i) for i in range(4))
    has_halo = jnp.where(lax.axis_index("ta") == 0, 0.0, 1.0)
    f_hi, f_lo = wide[:256], wide[256:512]
    i_hi, i_lo = wide[512:768], wide[768:1024]
    size = min(len(series), 8)
    for g in range(0, len(series), size):
        staged = []
        for i in range(g, g + size, 2):
            blocks = [h_ref[pl.ds(b * ROWS, ROWS), :] for b in (i, i + 1)]
            staged += first_stage(blocks, w1, twh_c * has_halo, twh_s * has_halo)
        spec = second_stage(jnp.concatenate(staged, axis=0), f_hi, f_lo)
        whole = []
        for i, s in enumerate(series[g : g + size]):
            before = parts(spec[i * ROWS : (i + 1) * ROWS])
            for c, other in enumerate((x0_ref, y0_ref)):
                re, im = mul_conj(parts(other[s]), before)
                whole.append(pre_ref[s, c] + jnp.concatenate([re, im], axis=1))
        back = second_stage(jnp.concatenate(whole, axis=0), i_hi, i_lo)
        for i, s in enumerate(series[g : g + size]):
            turned = []
            for c in range(2):
                re, im = parts(back[(2 * i + c) * ROWS : (2 * i + c + 1) * ROWS])
                turned.append(jnp.concatenate([re * tw_c - im * tw_s, re * tw_s + im * tw_c], axis=0))
            hi, lo = split(jnp.concatenate(turned, axis=1))
            lags = dot(w4, jnp.concatenate([hi, hi, lo], axis=0))
            for c in range(2):
                for low in range(4):
                    out_ref[pl.ds(c * 64 + s // 8 * 32 + low * 8 + s % 8, 8, stride=128), :] = lags[
                        low * 8 : low * 8 + 8, c * LANES : (c + 1) * LANES
                    ]


VMEM = pl.BlockSpec(memory_space=pltpu.VMEM)
SMEM = pl.BlockSpec(memory_space=pltpu.SMEM)
ANY = pl.BlockSpec(memory_space=pl.ANY)
RING = [(i, (i + 1) % 8) for i in range(8)]


def flat(array):
    return array.reshape(2, 8, -1, LANES).transpose(0, 2, 1, 3).reshape(-1, LANES)


def floats(*shape):
    return jax.ShapeDtypeStruct(shape, F32)


def cost(flops, nbytes):
    return pl.CostEstimate(flops=flops, bytes_accessed=nbytes, transcendentals=0)


def body(series, index_series, assign):
    wide = tables()
    params = pltpu.CompilerParams(vmem_limit_bytes=40 * 1024 * 1024)
    x, y = flat(series), flat(index_series)
    pieces = [range(*ends) for ends in zip(SPLITS, SPLITS[1:])]
    sent = []
    for series in pieces:
        sent.append(
            pl.pallas_call(
                functools.partial(tails_kernel, series),
                out_shape=floats(len(series) * ROWS, LANES),
                in_specs=[VMEM] + [ANY] * len(sent[-1:]),
                out_specs=VMEM,
                compiler_params=params,
                cost_estimate=cost(1_000_000_000, 2_000_000),
                name="tails",
            )(x, *sent[-1:])
        )
    halos = [lax.ppermute(tail, "ta", RING) for tail in sent]
    wide = jnp.asarray(wide)
    spec = (16, ROWS, 2 * LANES)
    local = pl.pallas_call(
        local_kernel,
        out_shape=(floats(16, 2, ROWS, 2 * LANES), floats(*spec), floats(*spec)),
        in_specs=[SMEM] + [VMEM] * 3,
        out_specs=(VMEM,) * 3,
        scratch_shapes=[pltpu.VMEM((1024, 2 * LANES), F32)],
        compiler_params=params,
        cost_estimate=cost(3_000_000_000, 3_000_000),
        name="local_terms",
    )(assign, x, y, wide)

    def lags(series, *operands):
        return pl.pallas_call(
            functools.partial(halo_kernel, series),
            out_shape=floats(1024, LANES),
            in_specs=[VMEM] * len(operands),
            out_specs=VMEM,
            input_output_aliases={5: 0} if len(operands) > 5 else {},
            compiler_params=params,
            cost_estimate=cost(1_000_000_000, 2_000_000),
            name="halo_and_lags",
        )(*operands)

    out = ()
    for series, halo in zip(pieces, halos):
        out = (lags(series, halo, *local, wide, *out),)
    (out,) = out
    shares = lax.all_to_all(out.reshape(8, 128, LANES), "ta", 0, 0, tiled=True)
    total = jnp.sum(shares, axis=0).reshape(2, 2, 4, 8, LANES)
    both = total.transpose(0, 1, 3, 2, 4).reshape(2, 16, 512)
    return both[0], both[1]


def solution(mesh):
    return jax.shard_map(
        body,
        mesh=mesh,
        in_specs=(P("sa", "ta"), P(None, "ta"), P()),
        out_specs=(P("sa", "ta"), P("sa", "ta")),
        check_vma=False,
    )
```

profile of v0, /device:TPU:2, one launch (start us, length us, event | category | flops | bytes accessed | tf_op | source)
XLA Modules:
  0.0 26.2 jit_solution(17414313861091313349)
XLA Ops:
  0.6 0.0 copy-start.1
  0.6 1.0 %copy-done.1 = f32[16,8192]{1,0:T(8,128)S(1)} copy-done((f32[16,8192]{1,0:T(8,128)S(1)}, f32[16,8192]{1,0:T(8,128)}, u32[]{:S(2)}) %copy-start.1) | copy-done | bytes 524312
  1.7 2.0 %collective-permute-start.2 = (f32[192,128]{1,0:T(8,128)S(1)}, f32[192,128]{1,0:T(8,128)S(1)}, u32[]{:S(2)}, u32[]{:S(2)}) collective-permute-start(f32[192,128]{1,0:T(8,128)S(1)} %tails.3.refs_0_), channel_id=1, source_target_pairs={{0,32},{32,64},{64,96},{96,128},{128,160},{160,192},{192,224},{224... | collective-permute-start | bytes 294920 | tf_op jit(solution)/shard_map/ppermute | solution.py:233
  3.7 0.0 copy-start
  3.7 0.0 copy-start.2
  3.7 0.0 copy-start.3
  3.7 1.2 %collective-permute-start.1 = (f32[192,128]{1,0:T(8,128)S(1)}, f32[192,128]{1,0:T(8,128)S(1)}, u32[]{:S(2)}, u32[]{:S(2)}) collective-permute-start(f32[192,128]{1,0:T(8,128)S(1)} %tails.4.refs_0_), channel_id=1, source_target_pairs={{0,32},{32,64},{64,96},{96,128},{128,160},{160,192},{192,224},{224... | collective-permute-start | bytes 294920 | tf_op jit(solution)/shard_map/ppermute | solution.py:233
  5.0 2.0 %collective-permute-start = (f32[128,128]{1,0:T(8,128)S(1)}, f32[128,128]{1,0:T(8,128)S(1)}, u32[]{:S(2)}, u32[]{:S(2)}) collective-permute-start(f32[128,128]{1,0:T(8,128)S(1)} %tails.5), channel_id=1, source_target_pairs={{0,32},{32,64},{64,96},{96,128},{128,160},{160,192},{192,224},{224... | collective-permute-start | bytes 196616 | tf_op jit(solution)/shard_map/ppermute | solution.py:233
  7.0 0.0 copy-done
  7.0 0.0 copy-done.2
  7.0 0.0 copy-done.3
  7.0 2.2 %local_terms.1 = (f32[16,2,32,256]{3,2,1,0:T(8,128)S(1)}, f32[16,32,256]{2,1,0:T(8,128)S(1)}, f32[16,32,256]{2,1,0:T(8,128)S(1)}) custom-call(s32[512]{0:T(512)S(1)} %copy-done.3, f32[1024,128]{1,0:T(8,128)S(1)} %bitcast.22, f32[1024,128]{1,0:T(8,128)S(1)} %bitcast.23, bf16[1408,256]{1,0:T(8,128)(2,1)S(1)} %copy-done), custom_call_target="tpu_custom_call" | custom-call | flops 3000000000 | bytes 3000000 | tf_op jit(solution)/shard_map/local_terms/pallas_call | solution.py:236
  9.2 0.6 %collective-permute-done.2.h_ref = f32[192,128]{1,0:T(8,128)S(1)} collective-permute-done((f32[192,128]{1,0:T(8,128)S(1)}, f32[192,128]{1,0:T(8,128)S(1)}, u32[]{:S(2)}, u32[]{:S(2)}) %collective-permute-start.2) | collective-permute-done | bytes 98336 | tf_op jit(solution)/shard_map/ppermute | solution.py:233
  9.8 1.0 %halo_and_lags.3.refs_0_ = f32[1024,128]{1,0:T(8,128)S(1)} custom-call(f32[192,128]{1,0:T(8,128)S(1)} %collective-permute-done.2.h_ref, f32[16,2,32,256]{3,2,1,0:T(8,128)S(1)} %get-tuple-element.5.pre_ref, f32[16,32,256]{2,1,0:T(8,128)S(1)} %get-tuple-element.6.x0_ref, f32[16,32,256]{2,1,0:T(8,128)S(1)} %get-tuple-element.7.y0_ref, bf16[1408,256]{1,0:T(8,128)(2,1)S(1)} %copy-done), custom_call_target="tpu_custom_call" | custom-call | flops 1000000000 | bytes 2000000 | tf_op jit(solution)/shard_map/halo_and_lags/pallas_call | solution.py:248
  10.8 0.9 %collective-permute-done.1.h_ref = f32[192,128]{1,0:T(8,128)S(1)} collective-permute-done((f32[192,128]{1,0:T(8,128)S(1)}, f32[192,128]{1,0:T(8,128)S(1)}, u32[]{:S(2)}, u32[]{:S(2)}) %collective-permute-start.1) | collective-permute-done | bytes 98336 | tf_op jit(solution)/shard_map/ppermute | solution.py:233
  11.7 1.0 %halo_and_lags.4.refs_0_ = f32[1024,128]{1,0:T(8,128)S(1)} custom-call(f32[192,128]{1,0:T(8,128)S(1)} %collective-permute-done.1.h_ref, f32[16,2,32,256]{3,2,1,0:T(8,128)S(1)} %get-tuple-element.5.pre_ref, f32[16,32,256]{2,1,0:T(8,128)S(1)} %get-tuple-element.6.x0_ref, f32[16,32,256]{2,1,0:T(8,128)S(1)} %get-tuple-element.7.y0_ref, ...), custom_call_target="tpu_custom_call", output_to_operand_aliasing={{}: (5, {})} | custom-call | flops 1000000000 | bytes 2000000 | tf_op jit(solution)/shard_map/halo_and_lags/pallas_call | solution.py:248
  12.8 0.0 collective-permute-done.h_ref
  12.8 0.9 %halo_and_lags.5 = f32[1024,128]{1,0:T(8,128)S(1)} custom-call(f32[128,128]{1,0:T(8,128)S(1)} %collective-permute-done.h_ref, f32[16,2,32,256]{3,2,1,0:T(8,128)S(1)} %get-tuple-element.5.pre_ref, f32[16,32,256]{2,1,0:T(8,128)S(1)} %get-tuple-element.6.x0_ref, f32[16,32,256]{2,1,0:T(8,128)S(1)} %get-tuple-element.7.y0_ref, ...), custom_call_target="tpu_custom_call", output_to_operand_aliasing={{}: (5, {})} | custom-call | flops 1000000000 | bytes 2000000 | tf_op jit(solution)/shard_map/halo_and_lags/pallas_call | solution.py:248
  13.6 11.9 %all_to_all.5 = f32[8,128,128]{2,1,0:T(8,128)S(1)} all-to-all(f32[8,128,128]{2,1,0:T(8,128)S(1)} %bitcast.18), channel_id=1, replica_groups=mesh['ta'=8,'sa'=32] {'ta'}, dimensions={0} | all-to-all | bytes 1048576 | tf_op jit(solution)/shard_map/all_to_all | solution.py:263
  25.6 0.6 %slice_bitcast_fusion = (f32[16,512]{1,0:T(8,128)}, f32[16,512]{1,0:T(8,128)}) fusion(f32[2,2,8,4,128]{4,2,3,1,0:T(8,128)S(1)} %bitcast.24), kind=kLoop, calls=%fused_computation | loop fusion | bytes 131072 | tf_op jit(solution)/shard_map/squeeze | solution.py:266
  (4 shorter events, 0.1 us)
Async XLA Ops:
  0.6 1.0 %copy-start.1 = (f32[16,8192]{1,0:T(8,128)S(1)}, f32[16,8192]{1,0:T(8,128)}, u32[]{:S(2)}) copy-start(f32[16,8192]{1,0:T(8,128)} %param.4) | copy-start | bytes 1572868
  1.7 8.1 %collective-permute-start.2 = (f32[192,128]{1,0:T(8,128)S(1)}, f32[192,128]{1,0:T(8,128)S(1)}, u32[]{:S(2)}, u32[]{:S(2)}) collective-permute-start(f32[192,128]{1,0:T(8,128)S(1)} %tails.3.refs_0_), channel_id=1, source_target_pairs={{0,32},{32,64},{64,96},{96,128},{128,160},{160,192},{192,224},{224... | collective-permute-start | bytes 294920 | tf_op jit(solution)/shard_map/ppermute | solution.py:233
  3.7 3.2 %copy-start = (bf16[1408,256]{1,0:T(8,128)(2,1)S(1)}, bf16[1408,256]{1,0:T(8,128)(2,1)}, u32[]{:S(2)}) copy-start(bf16[1408,256]{1,0:T(8,128)(2,1)} %constant.4.clone.wide) | copy-start | bytes 2162692
  3.7 3.2 %copy-start.2 = (f32[16,8192]{1,0:T(8,128)S(1)}, f32[16,8192]{1,0:T(8,128)}, u32[]{:S(2)}) copy-start(f32[16,8192]{1,0:T(8,128)} %param.5) | copy-start | bytes 1572868
  3.7 3.2 %copy-start.3 = (s32[512]{0:T(512)S(1)}, s32[512]{0:T(512)}, u32[]{:S(2)}) copy-start(s32[512]{0:T(512)} %assign_ref.1) | copy-start | bytes 6148
  3.7 8.0 %collective-permute-start.1 = (f32[192,128]{1,0:T(8,128)S(1)}, f32[192,128]{1,0:T(8,128)S(1)}, u32[]{:S(2)}, u32[]{:S(2)}) collective-permute-start(f32[192,128]{1,0:T(8,128)S(1)} %tails.4.refs_0_), channel_id=1, source_target_pairs={{0,32},{32,64},{64,96},{96,128},{128,160},{160,192},{192,224},{224... | collective-permute-start | bytes 294920 | tf_op jit(solution)/shard_map/ppermute | solution.py:233
  5.0 7.8 %collective-permute-start = (f32[128,128]{1,0:T(8,128)S(1)}, f32[128,128]{1,0:T(8,128)S(1)}, u32[]{:S(2)}, u32[]{:S(2)}) collective-permute-start(f32[128,128]{1,0:T(8,128)S(1)} %tails.5), channel_id=1, source_target_pairs={{0,32},{32,64},{64,96},{96,128},{128,160},{160,192},{192,224},{224... | collective-permute-start | bytes 196616 | tf_op jit(solution)/shard_map/ppermute | solution.py:233
where the time goes:
time: 26.4 us; the launch traced here: 26.2 us
  blocking collectives  11.9 us (45%)
  starting transfers between devices  5.19 us (20%)
  Pallas kernels  5.18 us (20%)
  local copies, waits for them, and re-layouts  1.68 us (6%)
  waiting for transfers between devices  1.51 us (6%)
  between operations  0.72 us (3%)
    all_to_all x1, blocking collectives, body(): shares = lax.all_to_all(out.reshape(8, 128, LANES), 'ta', 0, 0, tiled=True)  11.9 us
    ppermute x3, starting transfers between devices, body(): halos = [lax.ppermute(tail, 'ta', RING) for tail in sent]  5.19 us
    pallas_call x3, Pallas kernels, lags(): pl.pallas_call(functools.partial(halo_kernel, series), out_shape=floats(1...  2.9 us
    pallas_call x1, Pallas kernels, body(): pl.pallas_call(local_kernel, out_shape=(floats(16, 2, ROWS, 2 * LANES), f...  2.23 us
    ppermute x3, waiting for transfers between devices, body(): halos = [lax.ppermute(tail, 'ta', RING) for tail in sent]  1.51 us
    unnamed x8, local copies, waits for them, and re-layouts  1.05 us
    squeeze x1, local copies, waits for them, and re-layouts, body(): return (both[0], both[1])  0.63 us
  transfers between devices with their start and end apart: 3, of which 2 were waited for; matrix products, arithmetic and copies ran while one was open for 0% of the time, Pallas kernels for 16%

commit v1 on v0

--- a/solution.py
+++ b/solution.py
@@ -17,7 +17,7 @@
 F32 = jnp.float32
 W1 = 1024
 W4 = W1 + 64
-SPLITS = (0, 6, 12, 16)
+SPLITS = (0, 4, 12, 16)
 TW = W4 + ROWS
 
 
@@ -194,6 +194,11 @@
                     ]
 
 
+def sum_kernel(shares_ref, auto_ref, cross_ref):
+    for c, ref in enumerate((auto_ref, cross_ref)):
+        ref[...] = sum(shares_ref[i, pl.ds(c * 64, 64), :] for i in range(8))
+
+
 VMEM = pl.BlockSpec(memory_space=pltpu.VMEM)
 SMEM = pl.BlockSpec(memory_space=pltpu.SMEM)
 ANY = pl.BlockSpec(memory_space=pl.ANY)
@@ -261,9 +266,16 @@
         out = (lags(series, halo, *local, wide, *out),)
     (out,) = out
     shares = lax.all_to_all(out.reshape(8, 128, LANES), "ta", 0, 0, tiled=True)
-    total = jnp.sum(shares, axis=0).reshape(2, 2, 4, 8, LANES)
-    both = total.transpose(0, 1, 3, 2, 4).reshape(2, 16, 512)
-    return both[0], both[1]
+    sums = pl.pallas_call(
+        sum_kernel,
+        out_shape=(floats(64, LANES),) * 2,
+        in_specs=[VMEM],
+        out_specs=(VMEM,) * 2,
+        compiler_params=params,
+        cost_estimate=cost(0, 600_000),
+        name="summed",
+    )(shares)
+    return tuple(s.reshape(2, 4, 8, LANES).transpose(0, 2, 1, 3).reshape(16, 512) for s in sums)
 
 
 def solution(mesh):

time: 26.4 us -> 26.3 us (level)
  Pallas kernels: 5.18 us -> 5.83 us
  local copies, waits for them, and re-layouts: 1.68 us -> 1.05 us
  blocking collectives: 11.9 us -> 11.5 us
  waiting for transfers between devices: 1.51 us -> 1.81 us
    pallas_call x0 -> x1, Pallas kernels: none -> 0.65 us  [body(): pl.pallas_call(sum_kernel, out_shape=(floats(64, LANES),) * 2, in_specs=[...]
    squeeze x1 -> x0, local copies, waits for them, and re-layouts: 0.63 us -> none  [body(): return (both[0], both[1])]
    all_to_all x1, blocking collectives: 11.9 us -> 11.5 us  [body(): shares = lax.all_to_all(out.reshape(8, 128, LANES), 'ta', 0, 0, tiled=True)]
    ppermute x3, waiting for transfers between devices: 1.51 us -> 1.81 us  [body(): halos = [lax.ppermute(tail, 'ta', RING) for tail in sent]]
  transfers between devices with their start and end apart: 3 -> 3, of which waited for: 2 -> 1; matrix products, arithmetic and copies ran while one was open for 0% -> 0% of each run, Pallas kernels for 16% -> 16%
where the time goes in v1:
time: 26.3 us; the launch traced here: 26.2 us
  blocking collectives  11.5 us (44%)
  Pallas kernels  5.83 us (22%)
  starting transfers between devices  5.19 us (20%)
  waiting for transfers between devices  1.81 us (7%)
  local copies, waits for them, and re-layouts  1.05 us (4%)
  between operations  0.72 us (3%)
    all_to_all x1, blocking collectives, body(): shares = lax.all_to_all(out.reshape(8, 128, LANES), 'ta', 0, 0, tiled=True)  11.5 us
    ppermute x3, starting transfers between devices, body(): halos = [lax.ppermute(tail, 'ta', RING) for tail in sent]  5.19 us
    pallas_call x3, Pallas kernels, lags(): pl.pallas_call(functools.partial(halo_kernel, series), out_shape=floats(1...  2.9 us
    pallas_call x1, Pallas kernels, body(): pl.pallas_call(local_kernel, out_shape=(floats(16, 2, ROWS, 2 * LANES), f...  2.23 us
    ppermute x3, waiting for transfers between devices, body(): halos = [lax.ppermute(tail, 'ta', RING) for tail in sent]  1.81 us
    unnamed x8, local copies, waits for them, and re-layouts  1.05 us
    pallas_call x1, Pallas kernels, body(): pl.pallas_call(sum_kernel, out_shape=(floats(64, LANES),) * 2, in_specs=[...  0.65 us
  transfers between devices with their start and end apart: 3, of which 1 were waited for; matrix products, arithmetic and copies ran while one was open for 0% of the time, Pallas kernels for 16%

profile of v1, /device:TPU:2, one launch (start us, length us, event | category | flops | bytes accessed | tf_op | source)
XLA Modules:
  0.0 26.2 jit_solution(8733543009165693981)
XLA Ops:
  0.6 0.0 copy-start.1
  0.6 1.0 %copy-done.1 = f32[16,8192]{1,0:T(8,128)S(1)} copy-done((f32[16,8192]{1,0:T(8,128)S(1)}, f32[16,8192]{1,0:T(8,128)}, u32[]{:S(2)}) %copy-start.1) | copy-done | bytes 524312
  1.7 2.0 %collective-permute-start.2 = (f32[128,128]{1,0:T(8,128)S(1)}, f32[128,128]{1,0:T(8,128)S(1)}, u32[]{:S(2)}, u32[]{:S(2)}) collective-permute-start(f32[128,128]{1,0:T(8,128)S(1)} %tails.3.refs_0_), channel_id=1, source_target_pairs={{0,32},{32,64},{64,96},{96,128},{128,160},{160,192},{192,224},{224... | collective-permute-start | bytes 196616 | tf_op jit(solution)/shard_map/ppermute | solution.py:238
  3.7 0.0 copy-start
  3.7 0.0 copy-start.2
  3.7 0.0 copy-start.3
  3.7 1.2 %collective-permute-start.1 = (f32[256,128]{1,0:T(8,128)S(1)}, f32[256,128]{1,0:T(8,128)S(1)}, u32[]{:S(2)}, u32[]{:S(2)}) collective-permute-start(f32[256,128]{1,0:T(8,128)S(1)} %tails.4.refs_0_), channel_id=1, source_target_pairs={{0,32},{32,64},{64,96},{96,128},{128,160},{160,192},{192,224},{224... | collective-permute-start | bytes 393224 | tf_op jit(solution)/shard_map/ppermute | solution.py:238
  5.0 2.0 %collective-permute-start = (f32[128,128]{1,0:T(8,128)S(1)}, f32[128,128]{1,0:T(8,128)S(1)}, u32[]{:S(2)}, u32[]{:S(2)}) collective-permute-start(f32[128,128]{1,0:T(8,128)S(1)} %tails.5), channel_id=1, source_target_pairs={{0,32},{32,64},{64,96},{96,128},{128,160},{160,192},{192,224},{224... | collective-permute-start | bytes 196616 | tf_op jit(solution)/shard_map/ppermute | solution.py:238
  7.0 0.0 copy-done
  7.0 0.0 copy-done.2
  7.0 0.0 copy-done.3
  7.0 2.2 %local_terms.1 = (f32[16,2,32,256]{3,2,1,0:T(8,128)S(1)}, f32[16,32,256]{2,1,0:T(8,128)S(1)}, f32[16,32,256]{2,1,0:T(8,128)S(1)}) custom-call(s32[512]{0:T(512)S(1)} %copy-done.3, f32[1024,128]{1,0:T(8,128)S(1)} %bitcast.25, f32[1024,128]{1,0:T(8,128)S(1)} %bitcast.26, bf16[1408,256]{1,0:T(8,128)(2,1)S(1)} %copy-done), custom_call_target="tpu_custom_call" | custom-call | flops 3000000000 | bytes 3000000 | tf_op jit(solution)/shard_map/local_terms/pallas_call | solution.py:241
  9.2 0.0 collective-permute-done.2.h_ref
  9.2 0.9 %halo_and_lags.3.refs_0_ = f32[1024,128]{1,0:T(8,128)S(1)} custom-call(f32[128,128]{1,0:T(8,128)S(1)} %collective-permute-done.2.h_ref, f32[16,2,32,256]{3,2,1,0:T(8,128)S(1)} %get-tuple-element.7.pre_ref, f32[16,32,256]{2,1,0:T(8,128)S(1)} %get-tuple-element.8.x0_ref, f32[16,32,256]{2,1,0:T(8,128)S(1)} %get-tuple-element.9.y0_ref, bf16[1408,256]{1,0:T(8,128)(2,1)S(1)} %copy-done), custom_call_target="tpu_custom_call" | custom-call | flops 1000000000 | bytes 2000000 | tf_op jit(solution)/shard_map/halo_and_lags/pallas_call | solution.py:253
  10.1 1.8 %collective-permute-done.1.h_ref = f32[256,128]{1,0:T(8,128)S(1)} collective-permute-done((f32[256,128]{1,0:T(8,128)S(1)}, f32[256,128]{1,0:T(8,128)S(1)}, u32[]{:S(2)}, u32[]{:S(2)}) %collective-permute-start.1) | collective-permute-done | bytes 131104 | tf_op jit(solution)/shard_map/ppermute | solution.py:238
  11.9 1.2 %halo_and_lags.4.refs_0_ = f32[1024,128]{1,0:T(8,128)S(1)} custom-call(f32[256,128]{1,0:T(8,128)S(1)} %collective-permute-done.1.h_ref, f32[16,2,32,256]{3,2,1,0:T(8,128)S(1)} %get-tuple-element.7.pre_ref, f32[16,32,256]{2,1,0:T(8,128)S(1)} %get-tuple-element.8.x0_ref, f32[16,32,256]{2,1,0:T(8,128)S(1)} %get-tuple-element.9.y0_ref, ...), custom_call_target="tpu_custom_call", output_to_operand_aliasing={{}: (5, {})} | custom-call | flops 1000000000 | bytes 2000000 | tf_op jit(solution)/shard_map/halo_and_lags/pallas_call | solution.py:253
  13.1 0.0 collective-permute-done.h_ref
  13.1 0.9 %halo_and_lags.5 = f32[1024,128]{1,0:T(8,128)S(1)} custom-call(f32[128,128]{1,0:T(8,128)S(1)} %collective-permute-done.h_ref, f32[16,2,32,256]{3,2,1,0:T(8,128)S(1)} %get-tuple-element.7.pre_ref, f32[16,32,256]{2,1,0:T(8,128)S(1)} %get-tuple-element.8.x0_ref, f32[16,32,256]{2,1,0:T(8,128)S(1)} %get-tuple-element.9.y0_ref, ...), custom_call_target="tpu_custom_call", output_to_operand_aliasing={{}: (5, {})} | custom-call | flops 1000000000 | bytes 2000000 | tf_op jit(solution)/shard_map/halo_and_lags/pallas_call | solution.py:253
  14.0 11.5 %all_to_all.5.shares_ref = f32[8,128,128]{2,1,0:T(8,128)S(1)} all-to-all(f32[8,128,128]{2,1,0:T(8,128)S(1)} %bitcast.21), channel_id=1, replica_groups=mesh['ta'=8,'sa'=32] {'ta'}, dimensions={0} | all-to-all | bytes 1048576 | tf_op jit(solution)/shard_map/all_to_all | solution.py:268
  25.5 0.6 %summed.1 = (f32[64,128]{1,0:T(8,128)}, f32[64,128]{1,0:T(8,128)}) custom-call(f32[8,128,128]{2,1,0:T(8,128)S(1)} %all_to_all.5.shares_ref), custom_call_target="tpu_custom_call" | custom-call | bytes 600000 | tf_op jit(solution)/shard_map/summed/pallas_call | solution.py:269
  (3 shorter events, 0.1 us)
Async XLA Ops:
  0.6 1.0 %copy-start.1 = (f32[16,8192]{1,0:T(8,128)S(1)}, f32[16,8192]{1,0:T(8,128)}, u32[]{:S(2)}) copy-start(f32[16,8192]{1,0:T(8,128)} %param.4) | copy-start | bytes 1572868
  1.7 7.5 %collective-permute-start.2 = (f32[128,128]{1,0:T(8,128)S(1)}, f32[128,128]{1,0:T(8,128)S(1)}, u32[]{:S(2)}, u32[]{:S(2)}) collective-permute-start(f32[128,128]{1,0:T(8,128)S(1)} %tails.3.refs_0_), channel_id=1, source_target_pairs={{0,32},{32,64},{64,96},{96,128},{128,160},{160,192},{192,224},{224... | collective-permute-start | bytes 196616 | tf_op jit(solution)/shard_map/ppermute | solution.py:238
  3.7 3.2 %copy-start = (bf16[1408,256]{1,0:T(8,128)(2,1)S(1)}, bf16[1408,256]{1,0:T(8,128)(2,1)}, u32[]{:S(2)}) copy-start(bf16[1408,256]{1,0:T(8,128)(2,1)} %constant.2.clone.wide) | copy-start | bytes 2162692
  3.7 3.2 %copy-start.2 = (f32[16,8192]{1,0:T(8,128)S(1)}, f32[16,8192]{1,0:T(8,128)}, u32[]{:S(2)}) copy-start(f32[16,8192]{1,0:T(8,128)} %param.5) | copy-start | bytes 1572868
  3.7 3.2 %copy-start.3 = (s32[512]{0:T(512)S(1)}, s32[512]{0:T(512)}, u32[]{:S(2)}) copy-start(s32[512]{0:T(512)} %assign_ref.1) | copy-start | bytes 6148
  3.7 8.1 %collective-permute-start.1 = (f32[256,128]{1,0:T(8,128)S(1)}, f32[256,128]{1,0:T(8,128)S(1)}, u32[]{:S(2)}, u32[]{:S(2)}) collective-permute-start(f32[256,128]{1,0:T(8,128)S(1)} %tails.4.refs_0_), channel_id=1, source_target_pairs={{0,32},{32,64},{64,96},{96,128},{128,160},{160,192},{192,224},{224... | collective-permute-start | bytes 393224 | tf_op jit(solution)/shard_map/ppermute | solution.py:238
  5.0 8.1 %collective-permute-start = (f32[128,128]{1,0:T(8,128)S(1)}, f32[128,128]{1,0:T(8,128)S(1)}, u32[]{:S(2)}, u32[]{:S(2)}) collective-permute-start(f32[128,128]{1,0:T(8,128)S(1)} %tails.5), channel_id=1, source_target_pairs={{0,32},{32,64},{64,96},{96,128},{128,160},{160,192},{192,224},{224... | collective-permute-start | bytes 196616 | tf_op jit(solution)/shard_map/ppermute | solution.py:238
